TPU v7x, 256 devices: a whole 4x4x8 slice. The times are simulated.
256 devices in a mesh: space: 16 (over x_hi, y, core), var: 2 (over x_lo), tm: 8 (over z).
Axes of the slice: x: 4 (x_hi: 2, x_lo: 2; x = x_hi * 2 + x_lo), y: 4, z: 8, core: 2. Of those that a mesh axis runs over, the one named last changes fastest.
Arguments:
- field: bfloat16 [128, 256, 32768], P('tm', 'var', 'space'), may hold values from -6 to 6
- factor_space: bfloat16 [32768, 128], P(('space', 'var', 'tm')), may hold values from -3 to 3
- factor_level: bfloat16 [256, 128], P('var'), may hold values from -3 to 3
- factor_time: bfloat16 [128, 128], P('tm'), may hold values from -3 to 3
Outputs:
- grad_space: float32 [32768, 128], P(('space', 'var', 'tm'))
- grad_level: float32 [256, 128], P('var')
- grad_time: float32 [128, 128], P('tm')
- loss: float32 [], replicated
All inputs are finite; a program needn't handle non-finite values.
Results may differ from a plain program's by a relative error of at most 0.00071.
Values may be sent and summed in bfloat16 or wider, within the bound.
A program may use at most 64 MiB of HBM per device.

v0:
```python
import jax
import jax.numpy as jnp
from jax import lax
from jax.sharding import PartitionSpec as P

J = 256


def on_device(field, factor_space, factor_level, factor_time):
    rows_own = factor_space.shape[0]
    columns = lax.all_gather(factor_space, ("var", "tm"), axis=0, tiled=True)
    level32 = factor_level.astype(jnp.float32)
    time32 = factor_time.astype(jnp.float32)
    khatri = (level32[None, :, :] * time32[:, None, :]).astype(jnp.bfloat16)
    model = jnp.einsum("kjr,ir->kji", khatri, columns, preferred_element_type=jnp.float32)
    misfit = model - field.astype(jnp.float32)
    misfit_b = misfit.astype(jnp.bfloat16)
    partial_total = jnp.sum(misfit * misfit)
    grad_a = jnp.einsum("kji,kjr->ir", misfit_b, khatri, preferred_element_type=jnp.float32)
    project = jnp.einsum("kji,ir->kjr", misfit_b, columns, preferred_element_type=jnp.float32)
    grad_b = jnp.sum(project * time32[:, None, :], axis=0)
    grad_c = jnp.sum(project * level32[None, :, :], axis=1)
    summed = lax.psum(grad_a, ("var", "tm"))
    offset = lax.axis_index(("var", "tm")) * rows_own
    owned = lax.dynamic_slice_in_dim(summed, offset, rows_own, 0)
    level_sum = lax.psum(grad_b, ("space", "tm"))
    time_sum, block_total = lax.psum((grad_c, partial_total), ("space", "var"))
    whole_total = lax.psum(block_total, "tm")
    count_i = rows_own * lax.axis_size(("space", "var", "tm"))
    count_k = field.shape[0] * lax.axis_size("tm")
    grad_space = owned / jnp.sqrt(jnp.float32(J * count_k))
    grad_level = level_sum / jnp.sqrt(jnp.float32(count_i * count_k))
    grad_time = time_sum / jnp.sqrt(jnp.float32(count_i * J))
    loss = 0.5 * whole_total / jnp.float32(count_i * J * count_k)
    return (grad_space, grad_level, grad_time, loss)


def solution(mesh):
    placed = (
        P("tm", "var", "space"),
        P(("space", "var", "tm"), None),
        P("var", None),
        P("tm", None),
    )
    return jax.shard_map(
        on_device,
        mesh=mesh,
        in_specs=placed,
        out_specs=(P(("space", "var", "tm"), None), P("var", None), P("tm", None), P()),
        check_vma=False,
    )
```

profile of v0, /device:TPU:1, one launch (start us, length us, event | category | flops | bytes accessed | tf_op | source)
XLA Modules:
  0.0 1304.8 jit_solution(1861976810886833387)
XLA Ops:
  7.2 0.0 all-reduce.6.cloned.1.call-start
  7.2 0.7 convert_element_type.16
  7.9 0.8 convert_element_type.15
  8.7 32.9 %all_gather.3 = bf16[2048,128]{1,0:T(8,128)(2,1)S(1)} all-gather(bf16[128,128]{1,0:T(8,128)(2,1)} %param.5), channel_id=1, replica_groups=mesh['space'=16,'var'=2,'tm'=8] {'var','tm'}, dimensions={0}, use_global_device_ids=true | all-gather | bytes 557056 | tf_op jit(solution)/shard_map/all_gather | solution.py:11
  41.6 7.5 multiply_reduce_fusion
  49.0 0.0 copy-start
  49.0 5.7 copy-done
  54.8 6.9 multiply_reduce_fusion.1
  61.7 0.0 all-reduce.6.cloned.1.call-update
  61.7 0.0 all-reduce.4.cloned.1.call-start
  61.7 12.3 convolution_bitcast_fusion
  74.1 0.0 all-reduce.4.cloned.1.call-update
  74.1 71.8 %all-reduce = (f32[16,128]{1,0:T(8,128)S(1)}, f32[]{:T(128)}) all-reduce(f32[16,128]{1,0:T(8,128)S(1)} %get-tuple-element.4, f32[]{:T(128)} %get-tuple-element.8), channel_id=1, replica_groups=mesh['space'=16,'var'=2,'tm'=8] {'space','var'}, use_global_device_ids=true, to_apply=%region_4.0 | all-reduce | flops 2049 | bytes 16392 | tf_op jit(solution)/shard_map/psum | solution.py:27
  145.9 12.4 psum.39
  159.0 0.6 broadcast_multiply_fusion.1
  159.6 988.6 %all-reduce.6.cloned.1.call-done = f32[128,128]{1,0:T(8,128)} async-done(((f32[128,128]{1,0:T(8,128)}), f32[128,128]{1,0:T(8,128)}) %all-reduce.6.cloned.1.call-update) | async-done | bytes 65552 | tf_op jit(solution)/shard_map/psum | solution.py:26
  1148.1 1.5 broadcast_multiply_fusion
  1149.6 145.7 %all-reduce.4.cloned.1.call-done = f32[2048,128]{1,0:T(8,128)} async-done(((f32[2048,128]{1,0:T(8,128)}), f32[2048,128]{1,0:T(8,128)}) %all-reduce.4.cloned.1.call-update) | async-done | bytes 1048592 | tf_op jit(solution)/shard_map/psum | solution.py:23
  1295.3 1.5 dynamic-slice_multiply_fusion
Async XLA Ops:
  7.2 1141.0 %all-reduce.6.cloned.1.call-start = ((), (), s32[]{:S(2)}) async-start(), calls=%async_computation.1 | async-start | bytes 131072 | tf_op jit(solution)/shard_map/psum | solution.py:26
  49.0 5.7 copy-start
  61.7 1233.6 %all-reduce.4.cloned.1.call-start = ((), (), s32[]{:S(2)}) async-start(), calls=%async_computation | async-start | bytes 2097152 | tf_op jit(solution)/shard_map/psum | solution.py:23
Sparse Core Ops, SparseCore 0:
  61.8 1086.2 all-reduce.5
  1150.9 144.3 all-reduce.3
where the time goes:
time: 1310 us; the launch traced here: 1300 us
  waiting for transfers between devices  1130 us (86%)
  blocking collectives  117 us (9%)
  matrix products  26.7 us (2%)
  between operations  15.8 us (1%)
    psum x1, waiting for transfers between devices, on_device(): level_sum = lax.psum(grad_b, ('space', 'tm'))  989 us
    psum x1, waiting for transfers between devices, on_device(): summed = lax.psum(grad_a, ('var', 'tm'))  146 us
    psum x1, blocking collectives, on_device(): time_sum, block_total = lax.psum((grad_c, partial_total), ('space', 'var'))  71.8 us
    all_gather x1, blocking collectives, on_device(): columns = lax.all_gather(factor_space, ('var', 'tm'), axis=0, tiled=True)  32.9 us
  transfers between devices with their start and end apart: 2, of which 2 were waited for; matrix products, arithmetic and copies ran while one was open for 1% of the time, Pallas kernels for 0%

commit v1 on v0

v1 whole, which is shorter than its diff:
```python
import functools

import jax
import jax.numpy as jnp
from jax import lax
from jax.experimental import pallas as pl
from jax.experimental.pallas import tpu as pltpu
from jax.sharding import PartitionSpec as P

MESH = pl.DeviceIdType.MESH
BF16, F32 = jnp.bfloat16, jnp.float32
NS, NV, NT = 16, 2, 8
CHUNK = 256


def offset_of(s):
    if isinstance(s, int):
        return (0, 4, 3, 5, 2, 6, 1, 7)[s]
    mag = 4 - s // 2
    signed = jnp.where(s % 2 == 0, mag, NT - mag)
    return jnp.where(s == 0, 0, jnp.where(s == 1, 4, signed))


def mirror(s):
    return (0, 1, 3, 2, 5, 4, 7, 6)[s]


def kernel(scales, field, s_ref, l_ref, t_ref, gs_ref, gl_ref, gt_ref, loss_ref,
           fbuf, ag, khat, khat_t, mb, proj, sq, part, xbuf, zs, zbuf,
           m1, r1, m2, r2, m3, r3, glf,
           fsem, agz_s, agz_r, agx_s, agx_r, rx_s, rx_r, rz_s, rz_r,
           p1_s, p1_r, p2_s, p2_r, p3_s, p3_r, px_s, px_r):
    sp, v, t = lax.axis_index("space"), lax.axis_index("var"), lax.axis_index("tm")
    partner = {"var": 1 - v}
    nk, nj = t_ref.shape[0], l_ref.shape[0]

    def zpeer(s):
        return lax.rem(t + offset_of(s), NT)

    def remote(src, dst, send, recv, dev):
        return pltpu.make_async_remote_copy(src_ref=src, dst_ref=dst, send_sem=send, recv_sem=recv,
                                            device_id=dev, device_id_type=MESH)

    def field_copy(s, h):
        owner = (v if h == 0 else 1 - v) * NT + lax.rem(t + offset_of(s), NT)
        cols = pl.ds(pl.multiple_of(owner * 128, 128), 128)
        return pltpu.make_async_copy(field.at[:, :, cols], fbuf.at[s, :, :, pl.ds(h * 128, 128)], fsem.at[s, h])

    barrier = pltpu.get_barrier_semaphore()
    for s in range(1, NT):
        pl.semaphore_signal(barrier, inc=1, device_id={"tm": zpeer(s)}, device_id_type=MESH)
    pl.semaphore_signal(barrier, inc=1, device_id=partner, device_id_type=MESH)
    for k in range(1, NS):
        pl.semaphore_signal(barrier, inc=1, device_id={"space": lax.rem(sp + k, NS)}, device_id_type=MESH)

    for s in range(NT):
        for h in range(2):
            field_copy(s, h).start()

    l32 = l_ref[...].astype(F32)
    t32 = t_ref[...].astype(F32)
    l32t, t32t = l32.T, t32.T
    for k in range(nk):
        khat[pl.ds(k * nj, nj), :] = (l32 * t32[k:k + 1, :]).astype(BF16)
        khat_t[:, pl.ds(k * nj, nj)] = (l32t * t32t[:, k:k + 1]).astype(BF16)
    ag[0, pl.ds(0, 128), :] = s_ref[...]
    proj[...] = jnp.zeros_like(proj)
    sq[...] = jnp.zeros_like(sq)

    pl.semaphore_wait(barrier, NT - 1 + 1 + NS - 1)

    def ag_z(s):
        m = mirror(s)
        return remote(s_ref, ag.at[m, pl.ds(0, 128)], agz_s.at[s], agz_r.at[m], {"tm": zpeer(s)})

    def ag_z_in(s):
        return remote(s_ref, ag.at[s, pl.ds(0, 128)], agz_s.at[s], agz_r.at[s], {"tm": zpeer(s)})

    def ag_x(s):
        src = s_ref if isinstance(s, int) and s == 0 else ag.at[s, pl.ds(0, 128)]
        return remote(src, ag.at[s, pl.ds(128, 128)], agx_s.at[s], agx_r.at[s], partner)

    ag_x(0).start()
    for s in range(1, NT):
        ag_z(s).start()
    for s in range(1, NT):
        ag_z_in(s).wait_recv()
        ag_x(s).start()

    def rs_x(s):
        return remote(part.at[s, 1], xbuf.at[s], rx_s.at[s], rx_r.at[s], partner)

    def step(s, carry):
        for h in range(2):
            field_copy(s, h).wait()
        ag_x_in = remote(s_ref, ag.at[s, pl.ds(128, 128)], agx_s.at[s], agx_r.at[s], partner)
        ag_x_in.wait_recv()
        sb = ag[s]
        per = CHUNK // nj
        for c in range(nk // per):
            rows = pl.ds(c * CHUNK, CHUNK)
            model = lax.dot_general(khat[rows, :], sb, (((1,), (1,)), ((), ())), preferred_element_type=F32)
            data = fbuf[s, pl.ds(c * per, per), :, :].reshape(CHUNK, 256).astype(F32)
            misfit = model - data
            sq[...] += jnp.sum((misfit * misfit).reshape(CHUNK // 8, 8, 256), axis=0)
            mb[rows, :] = misfit.astype(BF16)
        grad = jnp.dot(khat_t[...], mb[...], preferred_element_type=F32)
        part[s, 0] = grad[:, :128]
        part[s, 1] = grad[:, 128:]
        rs_x(s).start()
        proj[...] += jnp.dot(mb[...], sb, preferred_element_type=F32)
        return carry

    lax.fori_loop(0, NT, step, 0)

    glf[...] = jnp.zeros_like(glf)
    gts = []
    for k in range(nk):
        pk = proj[pl.ds(k * nj, nj), :]
        glf[...] += pk * t32[k:k + 1, :]
        gts.append(jnp.sum(pk * l32, axis=0, keepdims=True))
    gt_part = jnp.concatenate(gts, axis=0)
    loss_part = sq[:, :128] + sq[:, 128:]
    for q in range(NS):
        m1[q, pl.ds(0, 8), :] = glf[pl.ds(q * 8, 8), :]
        m1[q, pl.ds(8, 16), :] = gt_part
        m1[q, pl.ds(24, 8), :] = loss_part

    def plane(k):
        return lax.rem(sp + k, NS)

    def p1(k):
        q = plane(k)
        return remote(m1.at[q], r1.at[sp], p1_s.at[k], p1_r.at[sp], {"space": q})

    def p1_in(k):
        q = plane(k)
        return remote(m1.at[q], r1.at[q], p1_s.at[k], p1_r.at[q], {"space": q})

    for k in range(1, NS):
        p1(k).start()
    r1[sp] = m1[sp]

    def rs_z(s):
        m = mirror(s)
        return remote(zs.at[s], zbuf.at[m], rz_s.at[s], rz_r.at[m], {"tm": zpeer(s)})

    def rs_z_in(s):
        return remote(zs.at[s], zbuf.at[s], rz_s.at[s], rz_r.at[s], {"tm": zpeer(s)})

    for s in (1, 2, 3, 4, 5, 6, 7):
        rs_x(s).wait_recv()
        zs[s] = part[s, 0] + xbuf[s]
        rs_z(s).start()
    rs_x(0).wait_recv()

    for k in range(1, NS):
        p1_in(k).wait_recv()
    plane_sum = r1[0]
    for q in range(1, NS):
        plane_sum = plane_sum + r1[q]
    m2[pl.ds(0, 8), :] = plane_sum[0:8, :]
    m2[pl.ds(8, 8), :] = plane_sum[24:32, :]
    m3[pl.ds(0, 16), :] = plane_sum[8:24, :]

    def p2(s):
        return remote(m2, r2.at[t], p2_s.at[s], p2_r.at[t], {"tm": zpeer(s)})

    def p2_in(s):
        return remote(m2, r2.at[zpeer(s)], p2_s.at[s], p2_r.at[zpeer(s)], {"tm": zpeer(s)})

    for s in range(1, NT):
        p2(s).start()
    r2[t] = m2[...]
    for s in range(1, NT):
        p2_in(s).wait_recv()
    tm_sum = r2[0]
    for q in range(1, NT):
        tm_sum = tm_sum + r2[q]
    m3[pl.ds(16, 8), :] = tm_sum[8:16, :]
    px = remote(m3, r3, px_s, px_r, partner)
    px.start()
    glf[pl.ds(pl.multiple_of(sp * 8, 8), 8), :] = tm_sum[0:8, :] * scales[1]

    def p3(k):
        rows = pl.ds(pl.multiple_of(sp * 8, 8), 8)
        return remote(glf.at[rows], glf.at[rows], p3_s.at[k], p3_r.at[sp], {"space": plane(k)})

    def p3_in(k):
        rows = pl.ds(pl.multiple_of(plane(k) * 8, 8), 8)
        return remote(glf.at[rows], glf.at[rows], p3_s.at[k], p3_r.at[plane(k)], {"space": plane(k)})

    for k in range(1, NS):
        p3(k).start()

    total = part[0, 0] + xbuf[0]
    for s in range(1, NT):
        rs_z_in(s).wait_recv()
        total = total + zbuf[s]
    gs_ref[...] = total.T * scales[0]

    px.wait_recv()
    both = m3[...] + r3[...]
    gt_ref[...] = both[0:16, :] * scales[2]
    loss_ref[0, 0] = jnp.sum(both[16:24, :]) * scales[3]
    for k in range(1, NS):
        p3_in(k).wait_recv()
    gl_ref[...] = glf[...]

    px.wait_send()
    for s in range(NT):
        remote(s_ref, ag.at[s, pl.ds(128, 128)], agx_s.at[s], agx_r.at[s], partner).wait_send()
        rs_x(s).wait_send()
    for s in range(1, NT):
        ag_z(s).wait_send()
        rs_z(s).wait_send()
        p2(s).wait_send()
    for k in range(1, NS):
        p1(k).wait_send()
        p3(k).wait_send()


def on_device(field, factor_space, factor_level, factor_time):
    nk, nj, ni = field.shape
    own = factor_space.shape[0]
    kj = nk * nj
    count_i, count_j, count_k = own * NS * NV * NT, nj * NV, nk * NT
    scales = (
        1.0 / (count_j * count_k) ** 0.5,
        1.0 / (count_i * count_k) ** 0.5,
        1.0 / (count_i * count_j) ** 0.5,
        0.5 / (count_i * count_j * count_k),
    )
    dma = pltpu.SemaphoreType.DMA
    vmem = pl.BlockSpec(memory_space=pltpu.VMEM)
    gs, gl, gt, loss = pl.pallas_call(
        functools.partial(kernel, scales),
        out_shape=(
            jax.ShapeDtypeStruct((own, 128), F32),
            jax.ShapeDtypeStruct((nj, 128), F32),
            jax.ShapeDtypeStruct((nk, 128), F32),
            jax.ShapeDtypeStruct((1, 1), F32),
        ),
        in_specs=[pl.BlockSpec(memory_space=pl.ANY), vmem, vmem, vmem],
        out_specs=(vmem, vmem, vmem, pl.BlockSpec(memory_space=pltpu.SMEM)),
        scratch_shapes=[
            pltpu.VMEM((NT, nk, nj, 256), BF16),
            pltpu.VMEM((NT, 256, 128), BF16),
            pltpu.VMEM((kj, 128), BF16),
            pltpu.VMEM((128, kj), BF16),
            pltpu.VMEM((kj, 256), BF16),
            pltpu.VMEM((kj, 128), F32),
            pltpu.VMEM((8, 256), F32),
            pltpu.VMEM((NT, 2, 128, 128), F32),
            pltpu.VMEM((NT, 128, 128), F32),
            pltpu.VMEM((NT, 128, 128), F32),
            pltpu.VMEM((NT, 128, 128), F32),
            pltpu.VMEM((NS, 32, 128), F32),
            pltpu.VMEM((NS, 32, 128), F32),
            pltpu.VMEM((16, 128), F32),
            pltpu.VMEM((NT, 16, 128), F32),
            pltpu.VMEM((24, 128), F32),
            pltpu.VMEM((24, 128), F32),
            pltpu.VMEM((nj, 128), F32),
            dma((NT, 2)),
            dma((NT,)), dma((NT,)), dma((NT,)), dma((NT,)),
            dma((NT,)), dma((NT,)), dma((NT,)), dma((NT,)),
            dma((NS,)), dma((NS,)), dma((NT,)), dma((NT,)), dma((NS,)), dma((NS,)),
            dma, dma,
        ],
        compiler_params=pltpu.CompilerParams(collective_id=0, has_side_effects=True,
                                             vmem_limit_bytes=40 * 2**20),
    )(field, factor_space, factor_level, factor_time)
    return gs, gl, gt, loss.reshape(())


def solution(mesh):
    placed = (
        P("tm", "var", "space"),
        P(("space", "var", "tm"), None),
        P("var", None),
        P("tm", None),
    )
    return jax.shard_map(
        on_device,
        mesh=mesh,
        in_specs=placed,
        out_specs=(P(("space", "var", "tm"), None), P("var", None), P("tm", None), P()),
        check_vma=False,
    )
```

time: 1310 us -> 60.1 us (0.05)
  waiting for transfers between devices: 1130 us -> 0 us
  blocking collectives: 117 us -> 0 us
  Pallas kernels: 0 us -> 50 us
  matrix products: 26.7 us -> 0 us
  between operations: 15.8 us -> 2.4 us
    psum x2 -> x0, waiting for transfers between devices: 1130 us -> none  [the longest x1 989 us: on_device(): level_sum = lax.psum(grad_b, ('space', 'tm'))]
    psum x2 -> x0, blocking collectives: 84.2 us -> none  [the longest x1 71.8 us: on_device(): time_sum, block_total = lax.psum((grad_c, partial_total), ('space', 'var'))]
    pallas_call x0 -> x1, Pallas kernels: none -> 50 us  [on_device(): pl.pallas_call(functools.partial(kernel, scales), out_shape=(jax.ShapeDty...]
    all_gather x1 -> x0, blocking collectives: 32.9 us -> none  [on_device(): columns = lax.all_gather(factor_space, ('var', 'tm'), axis=0, tiled=True)]
    dot_general x3 -> x0, matrix products: 26.7 us -> none  [the longest x1 12.3 us: on_device(): jnp.einsum('kji,kjr->ir', misfit_b, khatri, preferred_element_type=jnp.fl...]
  transfers between devices with their start and end apart: 2 -> 0, of which waited for: 2 -> 0; matrix products, arithmetic and copies ran while one was open for 1% -> 0% of each run, Pallas kernels for 0% -> 0%
where the time goes in v1:
time: 60.1 us; the launch traced here: 59.8 us
  Pallas kernels  50 us (83%)
  local copies, waits for them, and re-layouts  7.43 us (12%)
  between operations  2.4 us (4%)
    pallas_call x1, Pallas kernels, on_device(): pl.pallas_call(functools.partial(kernel, scales), out_shape=(jax.ShapeDty...  50 us
    unnamed x11, local copies, waits for them, and re-layouts  7.43 us

profile of v1, /device:TPU:1, one launch (start us, length us, event | category | flops | bytes accessed | tf_op | source)
XLA Modules:
  0.0 59.8 jit_solution(6455513300617443733)
XLA Ops:
  0.6 0.0 copy-start
  0.6 3.4 %copy-done = bf16[16,128,2048]{2,1,0:T(8,128)(2,1)S(1)} copy-done((bf16[16,128,2048]{2,1,0:T(8,128)(2,1)S(1)}, bf16[16,128,2048]{2,1,0:T(8,128)(2,1)}, u32[]{:S(2)}) %copy-start) | copy-done | bytes 8388632
  4.0 0.0 copy-start.1
  4.0 0.8 %copy-done.1 = bf16[128,128]{1,0:T(8,128)(2,1)S(1)} copy-done((bf16[128,128]{1,0:T(8,128)(2,1)S(1)}, bf16[128,128]{1,0:T(8,128)(2,1)}, u32[]{:S(2)}) %copy-start.1) | copy-done | bytes 32792
  4.8 0.0 copy-start.2
  4.8 0.8 %copy-done.2 = bf16[128,128]{1,0:T(8,128)(2,1)S(1)} copy-done((bf16[128,128]{1,0:T(8,128)(2,1)S(1)}, bf16[128,128]{1,0:T(8,128)(2,1)}, u32[]{:S(2)}) %copy-start.2) | copy-done | bytes 32792
  5.5 0.0 copy-start.3
  5.5 0.7 %copy-done.3 = bf16[16,128]{1,0:T(8,128)(2,1)S(1)} copy-done((bf16[16,128]{1,0:T(8,128)(2,1)S(1)}, bf16[16,128]{1,0:T(8,128)(2,1)}, u32[]{:S(2)}) %copy-start.3) | copy-done | bytes 4120
  6.2 50.0 %shard_map.75 = (f32[128,128]{1,0:T(8,128)S(1)}, f32[128,128]{1,0:T(8,128)S(1)}, f32[16,128]{1,0:T(8,128)S(1)}, f32[1,1]{1,0:T(1,128)}) custom-call(bf16[16,128,2048]{2,1,0:T(8,128)(2,1)S(1)} %copy-done, bf16[128,128]{1,0:T(8,128)(2,1)S(1)} %copy-done.1, bf16[128,128]{1,0:T(8,128)(2,1)S(1)} %copy-done.2, bf16[16,128]{1,0:T(8,128)(2,1)S(1)} %copy-done.3), custom_call_target="tpu_custom_call" | custom-call | tf_op jit(solution)/shard_map/pallas_call | solution.py:236
  56.2 0.6 %copy.12 = f32[128,128]{1,0:T(8,128)} copy(f32[128,128]{1,0:T(8,128)S(1)} %get-tuple-element.16) | data formatting | bytes 131072
  56.9 0.6 %copy.13 = f32[128,128]{1,0:T(8,128)} copy(f32[128,128]{1,0:T(8,128)S(1)} %get-tuple-element.17) | data formatting | bytes 131072
  57.5 0.6 copy.14
Async XLA Ops:
  0.6 3.4 %copy-start = (bf16[16,128,2048]{2,1,0:T(8,128)(2,1)S(1)}, bf16[16,128,2048]{2,1,0:T(8,128)(2,1)}, u32[]{:S(2)}) copy-start(bf16[16,128,2048]{2,1,0:T(8,128)(2,1)} %field.1) | copy-start | bytes 25165828
  4.0 0.8 %copy-start.1 = (bf16[128,128]{1,0:T(8,128)(2,1)S(1)}, bf16[128,128]{1,0:T(8,128)(2,1)}, u32[]{:S(2)}) copy-start(bf16[128,128]{1,0:T(8,128)(2,1)} %s_ref.1) | copy-start | bytes 98308
  4.8 0.8 %copy-start.2 = (bf16[128,128]{1,0:T(8,128)(2,1)S(1)}, bf16[128,128]{1,0:T(8,128)(2,1)}, u32[]{:S(2)}) copy-start(bf16[128,128]{1,0:T(8,128)(2,1)} %l_ref.1) | copy-start | bytes 98308
  5.5 0.7 %copy-start.3 = (bf16[16,128]{1,0:T(8,128)(2,1)S(1)}, bf16[16,128]{1,0:T(8,128)(2,1)}, u32[]{:S(2)}) copy-start(bf16[16,128]{1,0:T(8,128)(2,1)} %t_ref.1) | copy-start | bytes 12292

commit v2 on v0

v2 whole, which is shorter than its diff:
```python
import functools

import jax
import jax.numpy as jnp
from jax import lax
from jax.experimental import pallas as pl
from jax.experimental.pallas import tpu as pltpu
from jax.sharding import PartitionSpec as P

MESH = pl.DeviceIdType.MESH
BF16, F32 = jnp.bfloat16, jnp.float32
NS, NV, NT = 16, 2, 8
NA, NX = 8, 2
NB = NX * NT
CHUNK = 512


def offset_of(s):
    if isinstance(s, int):
        return (0, 4, 3, 5, 2, 6, 1, 7)[s]
    mag = NT // 2 - s // 2
    signed = jnp.where(s % 2 == 0, mag, NT - mag)
    return jnp.where(s == 0, 0, jnp.where(s == 1, NT // 2, signed))


def mirror(s):
    return (0, 1, 3, 2, 5, 4, 7, 6)[s]


def kernel(scales, field, s_hbm, l_hbm, t_hbm, gs_ref, gl_ref, gt_ref, loss_ref,
           s_ref, l_ref, t_ref, fbuf, ag, khat, khat_t, mb, proj, sq, part, xbuf, zs, zbuf, rbuf, tbuf, hbuf,
           glf, r1, g1, q1, m2, r2, g2, q2, m3, r3, glo,
           isem, fsem, agz_s, agz_r, agx_s, agx_r, rx_s, rx_r, rz_s, rz_r, rr_s, rr_r, rh_s, rh_r,
           a1_s, a1_r, b1_s, b1_r, a2_s, a2_r, b2_s, b2_r, a3_s, a3_r, b3_s, b3_r):
    sp, v, t = lax.axis_index("space"), lax.axis_index("var"), lax.axis_index("tm")
    xh, a = sp // NA, sp % NA
    xc = xh * NV + v
    b = xh * NT + t
    partner = {"var": 1 - v}
    nk, nj = t_ref.shape[0], l_ref.shape[0]

    def zpeer(s):
        return lax.rem(t + offset_of(s), NT)

    def apeer(k):
        return lax.rem(a + k, NA)

    def a_id(k):
        return {"space": xh * NA + apeer(k)}

    def bpeer(k):
        return lax.rem(xh + k // NT, NX) * NT + lax.rem(t + k, NT)

    def b_id(k):
        return {"space": lax.rem(xh + k // NT, NX) * NA + a, "tm": lax.rem(t + k, NT)}

    def xpeer(k):
        return lax.rem(xc + k, NX * NV)

    def x_id(k):
        return {"space": xpeer(k) // NV * NA + a, "var": xpeer(k) % NV}

    def remote(src, dst, send, recv, dev):
        return pltpu.make_async_remote_copy(src_ref=src, dst_ref=dst, send_sem=send, recv_sem=recv,
                                            device_id=dev, device_id_type=MESH)

    small = [pltpu.make_async_copy(x, y, isem.at[i])
             for i, (x, y) in enumerate(((l_hbm, l_ref), (t_hbm, t_ref), (s_hbm, s_ref)))]
    for copy in small:
        copy.start()

    barrier = pltpu.get_barrier_semaphore()
    for k in range(1, NB):
        pl.semaphore_signal(barrier, inc=1, device_id=b_id(k), device_id_type=MESH)
    pl.semaphore_signal(barrier, inc=1, device_id=partner, device_id_type=MESH)
    pl.semaphore_signal(barrier, inc=1, device_id={"space": (1 - xh) * NA + a, "var": 1 - v}, device_id_type=MESH)
    for k in range(1, NA):
        pl.semaphore_signal(barrier, inc=1, device_id=a_id(k), device_id_type=MESH)

    def turn_of(i):
        if isinstance(i, int):
            return ((0, 0), (0, 1), (1, 0), (0, 2), (1, 1), (0, 3), (1, 2), (1, 3))[i]
        w = jnp.where(i == 7, 1, jnp.where(i == 0, 0, 1 - i % 2))
        return w, jnp.where(w == 1, (i - 1) // 2, (i + 1) // 2)

    def field_copy(i, h):
        w, p = turn_of(i)
        own = v + w * (1 - 2 * v)
        owner = own * NT + lax.rem(t + offset_of(2 * p + h), NT)
        cols = pl.ds(pl.multiple_of(owner * 128, 128), 128)
        return pltpu.make_async_copy(field.at[:, :, cols], fbuf.at[i, :, :, pl.ds(h * 128, 128)], fsem.at[i, h])

    for i in range(NT):
        for h in range(2):
            field_copy(i, h).start()

    for copy in small:
        copy.wait()
    l32 = l_ref[...].astype(F32)
    t32 = t_ref[...].astype(F32)
    l32t, t32t = l32.T, t32.T
    for k in range(nk):
        khat[pl.ds(k * nj, nj), :] = (l32 * t32[k:k + 1, :]).astype(BF16)
        khat_t[:, pl.ds(k * nj, nj)] = (l32t * t32t[:, k:k + 1]).astype(BF16)
    ag[0, 0, pl.ds(0, 128), :] = s_ref[...]
    proj[...] = jnp.zeros_like(proj)
    sq[...] = jnp.zeros_like(sq)

    pl.semaphore_wait(barrier, NB - 1 + 2 + NA - 1)

    def slot(w, s):
        return ag.at[w, s // 2, pl.ds((s % 2) * 128, 128)]

    def ag_z(s):
        return remote(s_ref, slot(0, mirror(s)), agz_s.at[s], agz_r.at[mirror(s)], {"tm": zpeer(s)})

    def ag_z_in(s):
        return remote(s_ref, slot(0, s), agz_s.at[s], agz_r.at[s], {"tm": zpeer(s)})

    def ag_x(p, h):
        rows = pl.ds(h * 128, 128)
        return remote(ag.at[0, p, rows], ag.at[1, p, rows], agx_s.at[p, h], agx_r.at[p, h], partner)

    remote(s_ref, slot(1, 0), agx_s.at[0, 0], agx_r.at[0, 0], partner).start()
    for s in range(1, NT):
        ag_z(s).start()

    def pass_on(p, h):
        s = 2 * p + h
        rows = pl.ds(h * 128, 128)
        remote(s_ref, ag.at[0, p, rows], agz_s.at[s], agz_r.at[s], partner).wait_recv()
        ag_x(p, h).start()

    def rs_x(p):
        two = pl.ds(2 * p, 2)
        return remote(part.at[1, two], xbuf.at[two], rx_s.at[p], rx_r.at[p], partner)

    rs_x1 = remote(part.at[1, 1], xbuf.at[1], rx_s.at[0], rx_r.at[0], partner)
    rs_x0 = remote(zs.at[0], xbuf.at[0], rx_s.at[3], rx_r.at[3], partner)

    def z_to(k):
        return {"tm": lax.rem(t + k, NT)}

    def near(s):
        m = mirror(s)
        return remote(part.at[0, s], zbuf.at[m], rz_s.at[s], rz_r.at[m], z_to(offset_of(s)))

    def relay(s):
        return remote(part.at[1, s], rbuf.at[s - 6], rr_s.at[s - 6], rr_r.at[s - 6], z_to(offset_of(s)))

    def half(h):
        rows = pl.ds(64 * h, 64)
        return remote(zs.at[1, rows], hbuf.at[h], rh_s.at[h], rh_r.at[h], z_to((2, 6)[h]))

    def short(s):
        return remote(zs.at[s], tbuf.at[s - 2], rz_s.at[s], rz_r.at[s], z_to((1, 7)[s - 2]))

    def last(s):
        m = mirror(s)
        return remote(zs.at[s], zbuf.at[m], rz_s.at[s], rz_r.at[m], z_to(offset_of(s)))

    def turn(i, carry):
        w, p = turn_of(i)

        @pl.when((i == 1) | (i == 3) | (i == 4))
        def _():
            for h in range(2):
                pass_on(jnp.where(i == 1, 1, i - 1), h)

        @pl.when(i == 7)
        def _():
            rs_x1.wait_recv()
            zs[1] = part[0, 1] + xbuf[1]
            for h in range(2):
                half(h).start()

        for h in range(2):
            field_copy(i, h).wait()

        @pl.when(w == 1)
        def _():
            for h in range(2):
                ag_x(p, h).wait_recv()

        sb = ag[w, p]
        per = CHUNK // nj
        acc = sq[...]
        for c in range(nk // per):
            rows = pl.ds(c * CHUNK, CHUNK)
            model = lax.dot_general(khat[rows, :], sb, (((1,), (1,)), ((), ())), preferred_element_type=F32)
            data = fbuf[i, pl.ds(c * per, per), :, :].reshape(CHUNK, 256).astype(F32)
            misfit = model - data
            acc = acc + jnp.sum((misfit * misfit).reshape(CHUNK // 8, 8, 256), axis=0)
            mb[rows, :] = misfit.astype(BF16)
        sq[...] = acc
        grad = jnp.dot(khat_t[...], mb[...], preferred_element_type=F32)
        part[w, 2 * p] = grad[:, :128]
        part[w, 2 * p + 1] = grad[:, 128:]

        @pl.when(i == 2)
        def _():
            rs_x1.start()

        @pl.when((i == 4) | (i == 6))
        def _():
            rs_x(p).start()

        @pl.when(i == 5)
        def _():
            for s in (6, 7):
                near(s).start()

        @pl.when(i == 7)
        def _():
            for s in (6, 7):
                relay(s).start()

        proj[...] += jnp.dot(mb[...], sb, preferred_element_type=F32)
        return carry

    pass_on(0, 1)
    lax.fori_loop(0, NT, turn, 0)

    ra = nj // NA

    def a_rows(q):
        return pl.ds(pl.multiple_of(q * ra, ra), ra)

    def level_rows(q):
        total = jnp.zeros((ra, 128), F32)
        for k in range(nk):
            rows = pl.ds(pl.multiple_of(k * nj + q * ra, ra), ra)
            total = total + proj[rows, :] * t32[k:k + 1, :]
        return total

    def a1(k):
        return remote(glf.at[apeer(k)], r1.at[a], a1_s.at[k], a1_r.at[a], a_id(k))

    def a1_in(k):
        return remote(glf.at[apeer(k)], r1.at[apeer(k)], a1_s.at[k], a1_r.at[apeer(k)], a_id(k))

    for k in range(1, NA):
        glf[apeer(k)] = level_rows(apeer(k))
        a1(k).start()
    r1[a] = level_rows(a)

    for k in range(nk):
        g1[pl.ds(k, 1), :] = jnp.sum(proj[pl.ds(k * nj, nj), :] * l32, axis=0, keepdims=True)
    g1[pl.ds(nk, 8), :] = sq[:, :128] + sq[:, 128:]

    def b1(k):
        return remote(g1, q1.at[a], b1_s.at[k], b1_r.at[a], a_id(k))

    def b1_in(k):
        return remote(g1, q1.at[apeer(k)], b1_s.at[k], b1_r.at[apeer(k)], a_id(k))

    for k in range(1, NA):
        b1(k).start()
    q1[a] = g1[...]

    rs_x(1).wait_recv()
    for s in (2, 3):
        zs[s] = part[0, s] + xbuf[s]
        short(s).start()

    for k in range(1, NA):
        a1_in(k).wait_recv()
    total = r1[0]
    for q in range(1, NA):
        total = total + r1[q]
    m2[...] = total

    def a2(k):
        return remote(m2, r2.at[b], a2_s.at[k], a2_r.at[b], b_id(k))

    def a2_in(k):
        return remote(m2, r2.at[bpeer(k)], a2_s.at[k], a2_r.at[bpeer(k)], b_id(k))

    for k in range(1, NB):
        a2(k).start()
    r2[b] = m2[...]

    for k in range(1, NA):
        b1_in(k).wait_recv()
    total = q1[0]
    for q in range(1, NA):
        total = total + q1[q]
    g2[...] = total

    def b2(k):
        return remote(g2, q2.at[xc], b2_s.at[k], b2_r.at[xc], x_id(k))

    def b2_in(k):
        return remote(g2, q2.at[xpeer(k)], b2_s.at[k], b2_r.at[xpeer(k)], x_id(k))

    for k in range(1, NX * NV):
        b2(k).start()
    q2[xc] = g2[...]

    for s in (6, 7):
        relay(s).wait_recv()
    zs[0] = part[1, 0] + rbuf[0] + rbuf[1]
    rs_x0.start()

    rs_x(2).wait_recv()
    for s in (4, 5):
        h = s - 4
        short(s - 2).wait_recv()
        half(h).wait_recv()
        zs[s] = part[0, s] + xbuf[s] + tbuf[h]
        rows = pl.ds(64 * h, 64)
        zs[s, rows] += hbuf[h]
        last(s).start()

    for k in range(1, NX * NV):
        b2_in(k).wait_recv()
    total = q2[0]
    for q in range(1, NX * NV):
        total = total + q2[q]
    gt_ref[...] = total[0:nk, :] * scales[2]
    m3[...] = total[nk:nk + 8, :]

    def b3(s):
        return remote(m3, r3.at[t], b3_s.at[s], b3_r.at[t], {"tm": zpeer(s)})

    def b3_in(s):
        return remote(m3, r3.at[zpeer(s)], b3_s.at[s], b3_r.at[zpeer(s)], {"tm": zpeer(s)})

    for s in range(1, NT):
        b3(s).start()
    r3[t] = m3[...]

    for k in range(1, NB):
        a2_in(k).wait_recv()
    total = r2[0]
    for q in range(1, NB):
        total = total + r2[q]
    glo[a_rows(a), :] = total * scales[1]

    def a3(k):
        return remote(glo.at[a_rows(a)], glo.at[a_rows(a)], a3_s.at[k], a3_r.at[a], a_id(k))

    def a3_in(k):
        rows = a_rows(apeer(k))
        return remote(glo.at[rows], glo.at[rows], a3_s.at[k], a3_r.at[apeer(k)], a_id(k))

    for k in range(1, NA):
        a3(k).start()

    rs_x0.wait_recv()
    total = part[0, 0] + xbuf[0]
    for s in (6, 7, 4, 5):
        remote(zs.at[s], zbuf.at[s], rz_s.at[s], rz_r.at[s], partner).wait_recv()
        total = total + zbuf[s]
    gs_ref[...] = total.T * scales[0]

    for s in range(1, NT):
        b3_in(s).wait_recv()
    total = r3[0]
    for q in range(1, NT):
        total = total + r3[q]
    loss_ref[0, 0] = jnp.sum(total) * scales[3]
    for k in range(1, NA):
        a3_in(k).wait_recv()
    gl_ref[...] = glo[...]

    rs_x0.wait_send()
    rs_x1.wait_send()
    for p in (1, 2):
        rs_x(p).wait_send()
    for h in range(2):
        half(h).wait_send()
        short(2 + h).wait_send()
        last(4 + h).wait_send()
        near(6 + h).wait_send()
        relay(6 + h).wait_send()
    for p in range(NT // 2):
        for h in range(2):
            ag_x(p, h).wait_send()
    for s in range(1, NT):
        ag_z(s).wait_send()
        b3(s).wait_send()
    for k in range(1, NA):
        a1(k).wait_send()
        b1(k).wait_send()
        a3(k).wait_send()
    for k in range(1, NB):
        a2(k).wait_send()
    for k in range(1, NX * NV):
        b2(k).wait_send()


def on_device(field, factor_space, factor_level, factor_time):
    nk, nj, ni = field.shape
    own = factor_space.shape[0]
    kj = nk * nj
    count_i, count_j, count_k = own * NS * NV * NT, nj * NV, nk * NT
    scales = (
        1.0 / (count_j * count_k) ** 0.5,
        1.0 / (count_i * count_k) ** 0.5,
        1.0 / (count_i * count_j) ** 0.5,
        0.5 / (count_i * count_j * count_k),
    )
    dma = pltpu.SemaphoreType.DMA
    vmem = pl.BlockSpec(memory_space=pltpu.VMEM)
    inputs = [pltpu.with_memory_space_constraint(x, pltpu.HBM)
              for x in (field, factor_space, factor_level, factor_time)]
    gs, gl, gt, loss = pl.pallas_call(
        functools.partial(kernel, scales),
        out_shape=(
            jax.ShapeDtypeStruct((own, 128), F32),
            jax.ShapeDtypeStruct((nj, 128), F32),
            jax.ShapeDtypeStruct((nk, 128), F32),
            jax.ShapeDtypeStruct((1, 1), F32),
        ),
        in_specs=[pl.BlockSpec(memory_space=pltpu.HBM)] * 4,
        out_specs=(vmem, vmem, vmem, pl.BlockSpec(memory_space=pltpu.SMEM)),
        scratch_shapes=[
            pltpu.VMEM((own, 128), BF16),
            pltpu.VMEM((nj, 128), BF16),
            pltpu.VMEM((nk, 128), BF16),
            pltpu.VMEM((NT, nk, nj, 256), BF16),
            pltpu.VMEM((NV, NT // 2, 256, 128), BF16),
            pltpu.VMEM((kj, 128), BF16),
            pltpu.VMEM((128, kj), BF16),
            pltpu.VMEM((kj, 256), BF16),
            pltpu.VMEM((kj, 128), F32),
            pltpu.VMEM((8, 256), F32),
            pltpu.VMEM((NV, NT, 128, 128), F32),
            pltpu.VMEM((NT, 128, 128), F32),
            pltpu.VMEM((NT, 128, 128), F32),
            pltpu.VMEM((NT, 128, 128), F32),
            pltpu.VMEM((2, 128, 128), F32),
            pltpu.VMEM((2, 128, 128), F32),
            pltpu.VMEM((2, 64, 128), F32),
            pltpu.VMEM((NA, nj // NA, 128), F32),
            pltpu.VMEM((NA, nj // NA, 128), F32),
            pltpu.VMEM((nk + 8, 128), F32),
            pltpu.VMEM((NA, nk + 8, 128), F32),
            pltpu.VMEM((nj // NA, 128), F32),
            pltpu.VMEM((NB, nj // NA, 128), F32),
            pltpu.VMEM((nk + 8, 128), F32),
            pltpu.VMEM((NX * NV, nk + 8, 128), F32),
            pltpu.VMEM((8, 128), F32),
            pltpu.VMEM((NT, 8, 128), F32),
            pltpu.VMEM((nj, 128), F32),
            dma((3,)), dma((NT, 2)),
            dma((NT,)), dma((NT,)), dma((NT // 2, 2)), dma((NT // 2, 2)),
            dma((NT // 2,)), dma((NT // 2,)), dma((NT,)), dma((NT,)),
            dma((2,)), dma((2,)), dma((2,)), dma((2,)),
            dma((NA,)), dma((NA,)), dma((NA,)), dma((NA,)),
            dma((NB,)), dma((NB,)), dma((NX * NV,)), dma((NX * NV,)),
            dma((NA,)), dma((NA,)), dma((NT,)), dma((NT,)),
        ],
        compiler_params=pltpu.CompilerParams(collective_id=0, has_side_effects=True,
                                             vmem_limit_bytes=40 * 2**20),
    )(*inputs)
    return gs, gl, gt, loss.reshape(())


def solution(mesh):
    placed = (
        P("tm", "var", "space"),
        P(("space", "var", "tm"), None),
        P("var", None),
        P("tm", None),
    )
    return jax.shard_map(
        on_device,
        mesh=mesh,
        in_specs=placed,
        out_specs=(P(("space", "var", "tm"), None), P("var", None), P("tm", None), P()),
        check_vma=False,
    )
```

time: 1310 us -> 53.3 us (0.04)
  waiting for transfers between devices: 1130 us -> 0 us
  blocking collectives: 117 us -> 0 us
  Pallas kernels: 0 us -> 49 us
  matrix products: 26.7 us -> 0 us
  between operations: 15.8 us -> 2.33 us
    psum x2 -> x0, waiting for transfers between devices: 1130 us -> none  [the longest x1 989 us: on_device(): level_sum = lax.psum(grad_b, ('space', 'tm'))]
    psum x2 -> x0, blocking collectives: 84.2 us -> none  [the longest x1 71.8 us: on_device(): time_sum, block_total = lax.psum((grad_c, partial_total), ('space', 'var'))]
    pallas_call x0 -> x1, Pallas kernels: none -> 49 us  [on_device(): pl.pallas_call(functools.partial(kernel, scales), out_shape=(jax.ShapeDty...]
    all_gather x1 -> x0, blocking collectives: 32.9 us -> none  [on_device(): columns = lax.all_gather(factor_space, ('var', 'tm'), axis=0, tiled=True)]
    dot_general x3 -> x0, matrix products: 26.7 us -> none  [the longest x1 12.3 us: on_device(): jnp.einsum('kji,kjr->ir', misfit_b, khatri, preferred_element_type=jnp.fl...]
  transfers between devices with their start and end apart: 2 -> 0, of which waited for: 2 -> 0; matrix products, arithmetic and copies ran while one was open for 1% -> 0% of each run, Pallas kernels for 0% -> 0%
where the time goes in v2:
time: 53.3 us; the launch traced here: 53.1 us
  Pallas kernels  49 us (92%)
  between operations  2.33 us (4%)
  local copies, waits for them, and re-layouts  1.86 us (3%)
    pallas_call x1, Pallas kernels, on_device(): pl.pallas_call(functools.partial(kernel, scales), out_shape=(jax.ShapeDty...  49 us
    unnamed x3, local copies, waits for them, and re-layouts  1.86 us

profile of v2, /device:TPU:1, one launch (start us, length us, event | category | flops | bytes accessed | tf_op | source)
XLA Modules:
  0.0 53.1 jit_solution(6250421105844815287)
XLA Ops:
  0.6 49.0 %shard_map.75 = (f32[128,128]{1,0:T(8,128)S(1)}, f32[128,128]{1,0:T(8,128)S(1)}, f32[16,128]{1,0:T(8,128)S(1)}, f32[1,1]{1,0:T(1,128)}) custom-call(bf16[16,128,2048]{2,1,0:T(8,128)(2,1)} %field.1, bf16[128,128]{1,0:T(8,128)(2,1)} %s_hbm.1, bf16[128,128]{1,0:T(8,128)(2,1)} %l_hbm.1, bf16[16,128]{1,0:T(8,128)(2,1)} %t_hbm.1), custom_call_target="tpu_custom_call" | custom-call | tf_op jit(solution)/shard_map/pallas_call | solution.py:408
  49.6 0.6 %copy.12 = f32[128,128]{1,0:T(8,128)} copy(f32[128,128]{1,0:T(8,128)S(1)} %get-tuple-element.16) | data formatting | bytes 131072
  50.2 0.6 %copy.13 = f32[128,128]{1,0:T(8,128)} copy(f32[128,128]{1,0:T(8,128)S(1)} %get-tuple-element.17) | data formatting | bytes 131072
  50.9 0.6 %copy.14 = f32[16,128]{1,0:T(8,128)} copy(f32[16,128]{1,0:T(8,128)S(1)} %get-tuple-element.18) | data formatting | bytes 16384

commit v3 on v2

--- a/solution.py
+++ b/solution.py
@@ -11,7 +11,6 @@
 BF16, F32 = jnp.bfloat16, jnp.float32
 NS, NV, NT = 16, 2, 8
 NA, NX = 8, 2
-NB = NX * NT
 CHUNK = 512
 
 
@@ -30,12 +29,11 @@
 def kernel(scales, field, s_hbm, l_hbm, t_hbm, gs_ref, gl_ref, gt_ref, loss_ref,
            s_ref, l_ref, t_ref, fbuf, ag, khat, khat_t, mb, proj, sq, part, xbuf, zs, zbuf, rbuf, tbuf, hbuf,
            glf, r1, g1, q1, m2, r2, g2, q2, m3, r3, glo,
-           isem, fsem, agz_s, agz_r, agx_s, agx_r, rx_s, rx_r, rz_s, rz_r, rr_s, rr_r, rh_s, rh_r,
+           isem, fsem, agh_s, agh_r, agz_s, agz_r, agx_s, agx_r, rx_s, rx_r, rz_s, rz_r, rr_s, rr_r, rh_s, rh_r,
            a1_s, a1_r, b1_s, b1_r, a2_s, a2_r, b2_s, b2_r, a3_s, a3_r, b3_s, b3_r):
     sp, v, t = lax.axis_index("space"), lax.axis_index("var"), lax.axis_index("tm")
     xh, a = sp // NA, sp % NA
     xc = xh * NV + v
-    b = xh * NT + t
     partner = {"var": 1 - v}
     nk, nj = t_ref.shape[0], l_ref.shape[0]
 
@@ -48,11 +46,11 @@
     def a_id(k):
         return {"space": xh * NA + apeer(k)}
 
-    def bpeer(k):
-        return lax.rem(xh + k // NT, NX) * NT + lax.rem(t + k, NT)
-
-    def b_id(k):
-        return {"space": lax.rem(xh + k // NT, NX) * NA + a, "tm": lax.rem(t + k, NT)}
+    def ppeer(k):
+        return lax.rem(sp + k, NS)
+
+    def p_id(k):
+        return {"space": ppeer(k)}
 
     def xpeer(k):
         return lax.rem(xc + k, NX * NV)
@@ -70,18 +68,20 @@
         copy.start()
 
     barrier = pltpu.get_barrier_semaphore()
-    for k in range(1, NB):
-        pl.semaphore_signal(barrier, inc=1, device_id=b_id(k), device_id_type=MESH)
+    for s in range(1, NT):
+        pl.semaphore_signal(barrier, inc=1, device_id={"tm": zpeer(s)}, device_id_type=MESH)
     pl.semaphore_signal(barrier, inc=1, device_id=partner, device_id_type=MESH)
     pl.semaphore_signal(barrier, inc=1, device_id={"space": (1 - xh) * NA + a, "var": 1 - v}, device_id_type=MESH)
-    for k in range(1, NA):
-        pl.semaphore_signal(barrier, inc=1, device_id=a_id(k), device_id_type=MESH)
+    for k in range(1, NS):
+        pl.semaphore_signal(barrier, inc=1, device_id=p_id(k), device_id_type=MESH)
 
     def turn_of(i):
         if isinstance(i, int):
-            return ((0, 0), (0, 1), (1, 0), (0, 2), (1, 1), (0, 3), (1, 2), (1, 3))[i]
-        w = jnp.where(i == 7, 1, jnp.where(i == 0, 0, 1 - i % 2))
-        return w, jnp.where(w == 1, (i - 1) // 2, (i + 1) // 2)
+            return ((0, 2), (0, 1), (1, 2), (0, 3), (0, 0), (1, 1), (1, 3), (1, 0))[i]
+        w = jnp.where((i == 2) | (i >= 5), 1, 0)
+        p = jnp.where((i == 3) | (i == 6), 3, 0)
+        p = jnp.where((i == 1) | (i == 5), 1, p)
+        return w, jnp.where((i == 0) | (i == 2), 2, p)
 
     def field_copy(i, h):
         w, p = turn_of(i)
@@ -106,7 +106,7 @@
     proj[...] = jnp.zeros_like(proj)
     sq[...] = jnp.zeros_like(sq)
 
-    pl.semaphore_wait(barrier, NB - 1 + 2 + NA - 1)
+    pl.semaphore_wait(barrier, NT - 1 + 2 + NS - 1)
 
     def slot(w, s):
         return ag.at[w, s // 2, pl.ds((s % 2) * 128, 128)]
@@ -122,8 +122,12 @@
         return remote(ag.at[0, p, rows], ag.at[1, p, rows], agx_s.at[p, h], agx_r.at[p, h], partner)
 
     remote(s_ref, slot(1, 0), agx_s.at[0, 0], agx_r.at[0, 0], partner).start()
-    for s in range(1, NT):
+    for s in (4, 5, 2, 3, 6, 7):
         ag_z(s).start()
+
+    def ag_half(h):
+        return remote(ag.at[0, 2, pl.ds(128 * h + 64 * h, 64)], ag.at[0, 0, pl.ds(128 + 64 * h, 64)],
+                      agh_s.at[h], agh_r.at[h], {"tm": lax.rem(t + (6, 2)[h], NT)})
 
     def pass_on(p, h):
         s = 2 * p + h
@@ -162,17 +166,16 @@
     def turn(i, carry):
         w, p = turn_of(i)
 
-        @pl.when((i == 1) | (i == 3) | (i == 4))
+        @pl.when((i == 1) | (i == 3))
         def _():
             for h in range(2):
-                pass_on(jnp.where(i == 1, 1, i - 1), h)
-
-        @pl.when(i == 7)
-        def _():
-            rs_x1.wait_recv()
-            zs[1] = part[0, 1] + xbuf[1]
+                pass_on(i, h)
+
+        @pl.when(i == 4)
+        def _():
             for h in range(2):
-                half(h).start()
+                ag_half(h).wait_recv()
+            ag_x(0, 1).start()
 
         for h in range(2):
             field_copy(i, h).wait()
@@ -197,31 +200,34 @@
         part[w, 2 * p] = grad[:, :128]
         part[w, 2 * p + 1] = grad[:, 128:]
 
-        @pl.when(i == 2)
-        def _():
-            rs_x1.start()
-
-        @pl.when((i == 4) | (i == 6))
+        @pl.when((i == 2) | (i == 5))
         def _():
             rs_x(p).start()
 
-        @pl.when(i == 5)
+        @pl.when(i == 3)
         def _():
             for s in (6, 7):
                 near(s).start()
 
-        @pl.when(i == 7)
+        @pl.when(i == 6)
         def _():
             for s in (6, 7):
                 relay(s).start()
 
+        @pl.when(i == 7)
+        def _():
+            rs_x1.start()
+
         proj[...] += jnp.dot(mb[...], sb, preferred_element_type=F32)
         return carry
 
-    pass_on(0, 1)
+    for h in range(2):
+        ag_z_in(4 + h).wait_recv()
+        ag_half(h).start()
+        ag_x(2, h).start()
     lax.fori_loop(0, NT, turn, 0)
 
-    ra = nj // NA
+    ra = nj // NS
 
     def a_rows(q):
         return pl.ds(pl.multiple_of(q * ra, ra), ra)
@@ -234,15 +240,15 @@
         return total
 
     def a1(k):
-        return remote(glf.at[apeer(k)], r1.at[a], a1_s.at[k], a1_r.at[a], a_id(k))
+        return remote(glf.at[ppeer(k)], r1.at[sp], a1_s.at[k], a1_r.at[sp], p_id(k))
 
     def a1_in(k):
-        return remote(glf.at[apeer(k)], r1.at[apeer(k)], a1_s.at[k], a1_r.at[apeer(k)], a_id(k))
-
-    for k in range(1, NA):
-        glf[apeer(k)] = level_rows(apeer(k))
+        return remote(glf.at[ppeer(k)], r1.at[ppeer(k)], a1_s.at[k], a1_r.at[ppeer(k)], p_id(k))
+
+    for k in range(1, NS):
+        glf[ppeer(k)] = level_rows(ppeer(k))
         a1(k).start()
-    r1[a] = level_rows(a)
+    r1[sp] = level_rows(sp)
 
     for k in range(nk):
         g1[pl.ds(k, 1), :] = jnp.sum(proj[pl.ds(k * nj, nj), :] * l32, axis=0, keepdims=True)
@@ -257,28 +263,37 @@
     for k in range(1, NA):
         b1(k).start()
     q1[a] = g1[...]
+
+    for s in (6, 7):
+        relay(s).wait_recv()
+    zs[0] = part[1, 0] + rbuf[0] + rbuf[1]
+    rs_x0.start()
 
     rs_x(1).wait_recv()
     for s in (2, 3):
         zs[s] = part[0, s] + xbuf[s]
         short(s).start()
-
-    for k in range(1, NA):
+    rs_x1.wait_recv()
+    zs[1] = part[0, 1] + xbuf[1]
+    for h in range(2):
+        half(h).start()
+
+    for k in range(1, NS):
         a1_in(k).wait_recv()
     total = r1[0]
-    for q in range(1, NA):
+    for q in range(1, NS):
         total = total + r1[q]
     m2[...] = total
 
-    def a2(k):
-        return remote(m2, r2.at[b], a2_s.at[k], a2_r.at[b], b_id(k))
-
-    def a2_in(k):
-        return remote(m2, r2.at[bpeer(k)], a2_s.at[k], a2_r.at[bpeer(k)], b_id(k))
-
-    for k in range(1, NB):
-        a2(k).start()
-    r2[b] = m2[...]
+    def a2(s):
+        return remote(m2, r2.at[t], a2_s.at[s], a2_r.at[t], {"tm": zpeer(s)})
+
+    def a2_in(s):
+        return remote(m2, r2.at[zpeer(s)], a2_s.at[s], a2_r.at[zpeer(s)], {"tm": zpeer(s)})
+
+    for s in range(1, NT):
+        a2(s).start()
+    r2[t] = m2[...]
 
     for k in range(1, NA):
         b1_in(k).wait_recv()
@@ -296,11 +311,6 @@
     for k in range(1, NX * NV):
         b2(k).start()
     q2[xc] = g2[...]
-
-    for s in (6, 7):
-        relay(s).wait_recv()
-    zs[0] = part[1, 0] + rbuf[0] + rbuf[1]
-    rs_x0.start()
 
     rs_x(2).wait_recv()
     for s in (4, 5):
@@ -312,6 +322,23 @@
         zs[s, rows] += hbuf[h]
         last(s).start()
 
+    for h in range(2):
+        ag_half(h).wait_send()
+        near(6 + h).wait_send()
+        relay(6 + h).wait_send()
+    for p in range(NT // 2):
+        for h in range(2):
+            ag_x(p, h).wait_send()
+    for s in range(2, NT):
+        ag_z(s).wait_send()
+    for k in range(1, NA):
+        b1(k).wait_send()
+    for k in range(1, NS):
+        a1(k).wait_send()
+    rs_x1.wait_send()
+    for p in (1, 2):
+        rs_x(p).wait_send()
+
     for k in range(1, NX * NV):
         b2_in(k).wait_recv()
     total = q2[0]
@@ -330,21 +357,21 @@
         b3(s).start()
     r3[t] = m3[...]
 
-    for k in range(1, NB):
-        a2_in(k).wait_recv()
+    for s in range(1, NT):
+        a2_in(s).wait_recv()
     total = r2[0]
-    for q in range(1, NB):
+    for q in range(1, NT):
         total = total + r2[q]
-    glo[a_rows(a), :] = total * scales[1]
+    glo[a_rows(sp), :] = total * scales[1]
 
     def a3(k):
-        return remote(glo.at[a_rows(a)], glo.at[a_rows(a)], a3_s.at[k], a3_r.at[a], a_id(k))
+        return remote(glo.at[a_rows(sp)], glo.at[a_rows(sp)], a3_s.at[k], a3_r.at[sp], p_id(k))
 
     def a3_in(k):
-        rows = a_rows(apeer(k))
-        return remote(glo.at[rows], glo.at[rows], a3_s.at[k], a3_r.at[apeer(k)], a_id(k))
-
-    for k in range(1, NA):
+        rows = a_rows(ppeer(k))
+        return remote(glo.at[rows], glo.at[rows], a3_s.at[k], a3_r.at[ppeer(k)], p_id(k))
+
+    for k in range(1, NS):
         a3(k).start()
 
     rs_x0.wait_recv()
@@ -360,34 +387,24 @@
     for q in range(1, NT):
         total = total + r3[q]
     loss_ref[0, 0] = jnp.sum(total) * scales[3]
-    for k in range(1, NA):
-        a3_in(k).wait_recv()
-    gl_ref[...] = glo[...]
-
+    for k in range(1, NX * NV):
+        b2(k).wait_send()
+    for s in range(1, NT):
+        a2(s).wait_send()
     rs_x0.wait_send()
-    rs_x1.wait_send()
-    for p in (1, 2):
-        rs_x(p).wait_send()
     for h in range(2):
         half(h).wait_send()
         short(2 + h).wait_send()
+    for h in range(2):
         last(4 + h).wait_send()
-        near(6 + h).wait_send()
-        relay(6 + h).wait_send()
-    for p in range(NT // 2):
-        for h in range(2):
-            ag_x(p, h).wait_send()
-    for s in range(1, NT):
-        ag_z(s).wait_send()
+    for s in range(1, NT):
         b3(s).wait_send()
-    for k in range(1, NA):
-        a1(k).wait_send()
-        b1(k).wait_send()
+    for k in range(1, NS):
+        a3_in(k).wait_recv()
+    gl_ref[...] = glo[...]
+
+    for k in range(1, NS):
         a3(k).wait_send()
-    for k in range(1, NB):
-        a2(k).wait_send()
-    for k in range(1, NX * NV):
-        b2(k).wait_send()
 
 
 def on_device(field, factor_space, factor_level, factor_time):
@@ -433,24 +450,24 @@
             pltpu.VMEM((2, 128, 128), F32),
             pltpu.VMEM((2, 128, 128), F32),
             pltpu.VMEM((2, 64, 128), F32),
-            pltpu.VMEM((NA, nj // NA, 128), F32),
-            pltpu.VMEM((NA, nj // NA, 128), F32),
+            pltpu.VMEM((NS, nj // NS, 128), F32),
+            pltpu.VMEM((NS, nj // NS, 128), F32),
             pltpu.VMEM((nk + 8, 128), F32),
             pltpu.VMEM((NA, nk + 8, 128), F32),
-            pltpu.VMEM((nj // NA, 128), F32),
-            pltpu.VMEM((NB, nj // NA, 128), F32),
+            pltpu.VMEM((nj // NS, 128), F32),
+            pltpu.VMEM((NT, nj // NS, 128), F32),
             pltpu.VMEM((nk + 8, 128), F32),
             pltpu.VMEM((NX * NV, nk + 8, 128), F32),
             pltpu.VMEM((8, 128), F32),
             pltpu.VMEM((NT, 8, 128), F32),
             pltpu.VMEM((nj, 128), F32),
-            dma((3,)), dma((NT, 2)),
+            dma((3,)), dma((NT, 2)), dma((2,)), dma((2,)),
             dma((NT,)), dma((NT,)), dma((NT // 2, 2)), dma((NT // 2, 2)),
             dma((NT // 2,)), dma((NT // 2,)), dma((NT,)), dma((NT,)),
             dma((2,)), dma((2,)), dma((2,)), dma((2,)),
-            dma((NA,)), dma((NA,)), dma((NA,)), dma((NA,)),
-            dma((NB,)), dma((NB,)), dma((NX * NV,)), dma((NX * NV,)),
-            dma((NA,)), dma((NA,)), dma((NT,)), dma((NT,)),
+            dma((NS,)), dma((NS,)), dma((NA,)), dma((NA,)),
+            dma((NT,)), dma((NT,)), dma((NX * NV,)), dma((NX * NV,)),
+            dma((NS,)), dma((NS,)), dma((NT,)), dma((NT,)),
         ],
         compiler_params=pltpu.CompilerParams(collective_id=0, has_side_effects=True,
                                              vmem_limit_bytes=40 * 2**20),

time: 53.3 us -> 50.2 us (0.942)
  Pallas kernels: 49 us -> 45.8 us
    pallas_call x1, Pallas kernels: 49 us -> 45.8 us  [on_device(): pl.pallas_call(functools.partial(kernel, scales), out_shape=(jax.ShapeDty...]
where the time goes in v3:
time: 50.2 us; the launch traced here: 50 us
  Pallas kernels  45.8 us (91%)
  between operations  2.33 us (5%)
  local copies, waits for them, and re-layouts  1.86 us (4%)
    pallas_call x1, Pallas kernels, on_device(): pl.pallas_call(functools.partial(kernel, scales), out_shape=(jax.ShapeDty...  45.8 us
    unnamed x3, local copies, waits for them, and re-layouts  1.86 us

profile of v3, /device:TPU:1, one launch (start us, length us, event | category | flops | bytes accessed | tf_op | source)
XLA Modules:
  0.0 50.0 jit_solution(12050188828592456568)
XLA Ops:
  0.6 45.8 %shard_map.75 = (f32[128,128]{1,0:T(8,128)S(1)}, f32[128,128]{1,0:T(8,128)S(1)}, f32[16,128]{1,0:T(8,128)S(1)}, f32[1,1]{1,0:T(1,128)}) custom-call(bf16[16,128,2048]{2,1,0:T(8,128)(2,1)} %field.1, bf16[128,128]{1,0:T(8,128)(2,1)} %s_hbm.1, bf16[128,128]{1,0:T(8,128)(2,1)} %l_hbm.1, bf16[16,128]{1,0:T(8,128)(2,1)} %t_hbm.1), custom_call_target="tpu_custom_call" | custom-call | tf_op jit(solution)/shard_map/pallas_call | solution.py:425
  46.5 0.6 %copy.12 = f32[128,128]{1,0:T(8,128)} copy(f32[128,128]{1,0:T(8,128)S(1)} %get-tuple-element.16) | data formatting | bytes 131072
  47.1 0.6 %copy.13 = f32[128,128]{1,0:T(8,128)} copy(f32[128,128]{1,0:T(8,128)S(1)} %get-tuple-element.17) | data formatting | bytes 131072
  47.7 0.6 %copy.14 = f32[16,128]{1,0:T(8,128)} copy(f32[16,128]{1,0:T(8,128)S(1)} %get-tuple-element.18) | data formatting | bytes 16384

commit v4 on v3

--- a/solution.py
+++ b/solution.py
@@ -27,9 +27,9 @@
 
 
 def kernel(scales, field, s_hbm, l_hbm, t_hbm, gs_ref, gl_ref, gt_ref, loss_ref,
-           s_ref, l_ref, t_ref, fbuf, ag, khat, khat_t, mb, proj, sq, part, xbuf, zs, zbuf, rbuf, tbuf, hbuf,
+           s_ref, l_ref, t_ref, fbuf, ag, khat, khat_t, mb, proj, sq, part, xbuf, zs, zbuf, rbuf, tbuf,
            glf, r1, g1, q1, m2, r2, g2, q2, m3, r3, glo,
-           isem, fsem, agh_s, agh_r, agz_s, agz_r, agx_s, agx_r, rx_s, rx_r, rz_s, rz_r, rr_s, rr_r, rh_s, rh_r,
+           isem, fsem, agh_s, agh_r, agz_s, agz_r, agx_s, agx_r, rx_s, rx_r, rz_s, rz_r, rr_s, rr_r,
            a1_s, a1_r, b1_s, b1_r, a2_s, a2_r, b2_s, b2_r, a3_s, a3_r, b3_s, b3_r):
     sp, v, t = lax.axis_index("space"), lax.axis_index("var"), lax.axis_index("tm")
     xh, a = sp // NA, sp % NA
@@ -152,9 +152,8 @@
     def relay(s):
         return remote(part.at[1, s], rbuf.at[s - 6], rr_s.at[s - 6], rr_r.at[s - 6], z_to(offset_of(s)))
 
-    def half(h):
-        rows = pl.ds(64 * h, 64)
-        return remote(zs.at[1, rows], hbuf.at[h], rh_s.at[h], rh_r.at[h], z_to((2, 6)[h]))
+    def far():
+        return remote(zs.at[1], zbuf.at[1], rz_s.at[1], rz_r.at[1], z_to(4))
 
     def short(s):
         return remote(zs.at[s], tbuf.at[s - 2], rz_s.at[s], rz_r.at[s], z_to((1, 7)[s - 2]))
@@ -227,7 +226,7 @@
         ag_x(2, h).start()
     lax.fori_loop(0, NT, turn, 0)
 
-    ra = nj // NS
+    ra = nj // NT
 
     def a_rows(q):
         return pl.ds(pl.multiple_of(q * ra, ra), ra)
@@ -240,15 +239,15 @@
         return total
 
     def a1(k):
-        return remote(glf.at[ppeer(k)], r1.at[sp], a1_s.at[k], a1_r.at[sp], p_id(k))
+        return remote(glf.at[zpeer(k)], r1.at[t], a1_s.at[k], a1_r.at[t], {"tm": zpeer(k)})
 
     def a1_in(k):
-        return remote(glf.at[ppeer(k)], r1.at[ppeer(k)], a1_s.at[k], a1_r.at[ppeer(k)], p_id(k))
-
-    for k in range(1, NS):
-        glf[ppeer(k)] = level_rows(ppeer(k))
+        return remote(glf.at[zpeer(k)], r1.at[zpeer(k)], a1_s.at[k], a1_r.at[zpeer(k)], {"tm": zpeer(k)})
+
+    for k in range(1, NT):
+        glf[zpeer(k)] = level_rows(zpeer(k))
         a1(k).start()
-    r1[sp] = level_rows(sp)
+    r1[t] = level_rows(t)
 
     for k in range(nk):
         g1[pl.ds(k, 1), :] = jnp.sum(proj[pl.ds(k * nj, nj), :] * l32, axis=0, keepdims=True)
@@ -275,25 +274,24 @@
         short(s).start()
     rs_x1.wait_recv()
     zs[1] = part[0, 1] + xbuf[1]
-    for h in range(2):
-        half(h).start()
-
-    for k in range(1, NS):
+    far().start()
+
+    for k in range(1, NT):
         a1_in(k).wait_recv()
     total = r1[0]
-    for q in range(1, NS):
+    for q in range(1, NT):
         total = total + r1[q]
     m2[...] = total
 
-    def a2(s):
-        return remote(m2, r2.at[t], a2_s.at[s], a2_r.at[t], {"tm": zpeer(s)})
-
-    def a2_in(s):
-        return remote(m2, r2.at[zpeer(s)], a2_s.at[s], a2_r.at[zpeer(s)], {"tm": zpeer(s)})
-
-    for s in range(1, NT):
-        a2(s).start()
-    r2[t] = m2[...]
+    def a2(k):
+        return remote(m2, r2.at[sp], a2_s.at[k], a2_r.at[sp], p_id(k))
+
+    def a2_in(k):
+        return remote(m2, r2.at[ppeer(k)], a2_s.at[k], a2_r.at[ppeer(k)], p_id(k))
+
+    for k in range(1, NS):
+        a2(k).start()
+    r2[sp] = m2[...]
 
     for k in range(1, NA):
         b1_in(k).wait_recv()
@@ -316,10 +314,7 @@
     for s in (4, 5):
         h = s - 4
         short(s - 2).wait_recv()
-        half(h).wait_recv()
         zs[s] = part[0, s] + xbuf[s] + tbuf[h]
-        rows = pl.ds(64 * h, 64)
-        zs[s, rows] += hbuf[h]
         last(s).start()
 
     for h in range(2):
@@ -333,7 +328,7 @@
         ag_z(s).wait_send()
     for k in range(1, NA):
         b1(k).wait_send()
-    for k in range(1, NS):
+    for k in range(1, NT):
         a1(k).wait_send()
     rs_x1.wait_send()
     for p in (1, 2):
@@ -357,26 +352,26 @@
         b3(s).start()
     r3[t] = m3[...]
 
-    for s in range(1, NT):
-        a2_in(s).wait_recv()
+    for k in range(1, NS):
+        a2_in(k).wait_recv()
     total = r2[0]
-    for q in range(1, NT):
+    for q in range(1, NS):
         total = total + r2[q]
-    glo[a_rows(sp), :] = total * scales[1]
+    glo[a_rows(t), :] = total * scales[1]
 
     def a3(k):
-        return remote(glo.at[a_rows(sp)], glo.at[a_rows(sp)], a3_s.at[k], a3_r.at[sp], p_id(k))
+        return remote(glo.at[a_rows(t)], glo.at[a_rows(t)], a3_s.at[k], a3_r.at[t], {"tm": zpeer(k)})
 
     def a3_in(k):
-        rows = a_rows(ppeer(k))
-        return remote(glo.at[rows], glo.at[rows], a3_s.at[k], a3_r.at[ppeer(k)], p_id(k))
-
-    for k in range(1, NS):
+        rows = a_rows(zpeer(k))
+        return remote(glo.at[rows], glo.at[rows], a3_s.at[k], a3_r.at[zpeer(k)], {"tm": zpeer(k)})
+
+    for k in range(1, NT):
         a3(k).start()
 
     rs_x0.wait_recv()
     total = part[0, 0] + xbuf[0]
-    for s in (6, 7, 4, 5):
+    for s in (6, 7, 4, 5, 1):
         remote(zs.at[s], zbuf.at[s], rz_s.at[s], rz_r.at[s], partner).wait_recv()
         total = total + zbuf[s]
     gs_ref[...] = total.T * scales[0]
@@ -389,21 +384,21 @@
     loss_ref[0, 0] = jnp.sum(total) * scales[3]
     for k in range(1, NX * NV):
         b2(k).wait_send()
-    for s in range(1, NT):
-        a2(s).wait_send()
+    for k in range(1, NS):
+        a2(k).wait_send()
     rs_x0.wait_send()
+    far().wait_send()
     for h in range(2):
-        half(h).wait_send()
         short(2 + h).wait_send()
     for h in range(2):
         last(4 + h).wait_send()
     for s in range(1, NT):
         b3(s).wait_send()
-    for k in range(1, NS):
+    for k in range(1, NT):
         a3_in(k).wait_recv()
     gl_ref[...] = glo[...]
 
-    for k in range(1, NS):
+    for k in range(1, NT):
         a3(k).wait_send()
 
 
@@ -449,13 +444,12 @@
             pltpu.VMEM((NT, 128, 128), F32),
             pltpu.VMEM((2, 128, 128), F32),
             pltpu.VMEM((2, 128, 128), F32),
-            pltpu.VMEM((2, 64, 128), F32),
-            pltpu.VMEM((NS, nj // NS, 128), F32),
-            pltpu.VMEM((NS, nj // NS, 128), F32),
+            pltpu.VMEM((NT, nj // NT, 128), F32),
+            pltpu.VMEM((NT, nj // NT, 128), F32),
             pltpu.VMEM((nk + 8, 128), F32),
             pltpu.VMEM((NA, nk + 8, 128), F32),
-            pltpu.VMEM((nj // NS, 128), F32),
-            pltpu.VMEM((NT, nj // NS, 128), F32),
+            pltpu.VMEM((nj // NT, 128), F32),
+            pltpu.VMEM((NS, nj // NT, 128), F32),
             pltpu.VMEM((nk + 8, 128), F32),
             pltpu.VMEM((NX * NV, nk + 8, 128), F32),
             pltpu.VMEM((8, 128), F32),
@@ -464,10 +458,10 @@
             dma((3,)), dma((NT, 2)), dma((2,)), dma((2,)),
             dma((NT,)), dma((NT,)), dma((NT // 2, 2)), dma((NT // 2, 2)),
             dma((NT // 2,)), dma((NT // 2,)), dma((NT,)), dma((NT,)),
-            dma((2,)), dma((2,)), dma((2,)), dma((2,)),
-            dma((NS,)), dma((NS,)), dma((NA,)), dma((NA,)),
-            dma((NT,)), dma((NT,)), dma((NX * NV,)), dma((NX * NV,)),
-            dma((NS,)), dma((NS,)), dma((NT,)), dma((NT,)),
+            dma((2,)), dma((2,)),
+            dma((NT,)), dma((NT,)), dma((NA,)), dma((NA,)),
+            dma((NS,)), dma((NS,)), dma((NX * NV,)), dma((NX * NV,)),
+            dma((NT,)), dma((NT,)), dma((NT,)), dma((NT,)),
         ],
         compiler_params=pltpu.CompilerParams(collective_id=0, has_side_effects=True,
                                              vmem_limit_bytes=40 * 2**20),

time: 50.2 us -> 49.3 us (0.982)
  Pallas kernels: 45.8 us -> 45 us
    pallas_call x1, Pallas kernels: 45.8 us -> 45 us  [on_device(): pl.pallas_call(functools.partial(kernel, scales), out_shape=(jax.ShapeDty...]
where the time goes in v4:
time: 49.3 us; the launch traced here: 49.2 us
  Pallas kernels  45 us (91%)
  between operations  2.33 us (5%)
  local copies, waits for them, and re-layouts  1.86 us (4%)
    pallas_call x1, Pallas kernels, on_device(): pl.pallas_call(functools.partial(kernel, scales), out_shape=(jax.ShapeDty...  45 us
    unnamed x3, local copies, waits for them, and re-layouts  1.86 us

profile of v4, /device:TPU:1, one launch (start us, length us, event | category | flops | bytes accessed | tf_op | source)
XLA Modules:
  0.0 49.2 jit_solution(2821686119033349043)
XLA Ops:
  0.6 45.0 %shard_map.75 = (f32[128,128]{1,0:T(8,128)S(1)}, f32[128,128]{1,0:T(8,128)S(1)}, f32[16,128]{1,0:T(8,128)S(1)}, f32[1,1]{1,0:T(1,128)}) custom-call(bf16[16,128,2048]{2,1,0:T(8,128)(2,1)} %field.1, bf16[128,128]{1,0:T(8,128)(2,1)} %s_hbm.1, bf16[128,128]{1,0:T(8,128)(2,1)} %l_hbm.1, bf16[16,128]{1,0:T(8,128)(2,1)} %t_hbm.1), custom_call_target="tpu_custom_call" | custom-call | tf_op jit(solution)/shard_map/pallas_call | solution.py:420
  45.6 0.6 %copy.12 = f32[128,128]{1,0:T(8,128)} copy(f32[128,128]{1,0:T(8,128)S(1)} %get-tuple-element.16) | data formatting | bytes 131072
  46.2 0.6 %copy.13 = f32[128,128]{1,0:T(8,128)} copy(f32[128,128]{1,0:T(8,128)S(1)} %get-tuple-element.17) | data formatting | bytes 131072
  46.9 0.6 %copy.14 = f32[16,128]{1,0:T(8,128)} copy(f32[16,128]{1,0:T(8,128)S(1)} %get-tuple-element.18) | data formatting | bytes 16384

commit v5 on v4

--- a/solution.py
+++ b/solution.py
@@ -77,10 +77,10 @@
 
     def turn_of(i):
         if isinstance(i, int):
-            return ((0, 2), (0, 1), (1, 2), (0, 3), (0, 0), (1, 1), (1, 3), (1, 0))[i]
+            return ((0, 2), (0, 3), (1, 2), (0, 1), (0, 0), (1, 3), (1, 1), (1, 0))[i]
         w = jnp.where((i == 2) | (i >= 5), 1, 0)
-        p = jnp.where((i == 3) | (i == 6), 3, 0)
-        p = jnp.where((i == 1) | (i == 5), 1, p)
+        p = jnp.where((i == 1) | (i == 5), 3, 0)
+        p = jnp.where((i == 3) | (i == 6), 1, p)
         return w, jnp.where((i == 0) | (i == 2), 2, p)
 
     def field_copy(i, h):
@@ -122,7 +122,7 @@
         return remote(ag.at[0, p, rows], ag.at[1, p, rows], agx_s.at[p, h], agx_r.at[p, h], partner)
 
     remote(s_ref, slot(1, 0), agx_s.at[0, 0], agx_r.at[0, 0], partner).start()
-    for s in (4, 5, 2, 3, 6, 7):
+    for s in (4, 5, 6, 7, 2, 3):
         ag_z(s).start()
 
     def ag_half(h):
@@ -168,7 +168,7 @@
         @pl.when((i == 1) | (i == 3))
         def _():
             for h in range(2):
-                pass_on(i, h)
+                pass_on(4 - i, h)
 
         @pl.when(i == 4)
         def _():
@@ -199,16 +199,16 @@
         part[w, 2 * p] = grad[:, :128]
         part[w, 2 * p + 1] = grad[:, 128:]
 
-        @pl.when((i == 2) | (i == 5))
+        @pl.when((i == 2) | (i == 6))
         def _():
             rs_x(p).start()
 
-        @pl.when(i == 3)
+        @pl.when(i == 1)
         def _():
             for s in (6, 7):
                 near(s).start()
 
-        @pl.when(i == 6)
+        @pl.when(i == 5)
         def _():
             for s in (6, 7):
                 relay(s).start()

time: 49.3 us -> 49.1 us (level)
  no operation moved by 1% of the time
where the time goes in v5:
time: 49.1 us; the launch traced here: 49 us
  Pallas kernels  44.8 us (91%)
  between operations  2.33 us (5%)
  local copies, waits for them, and re-layouts  1.86 us (4%)
    pallas_call x1, Pallas kernels, on_device(): pl.pallas_call(functools.partial(kernel, scales), out_shape=(jax.ShapeDty...  44.8 us
    unnamed x3, local copies, waits for them, and re-layouts  1.86 us

profile of v5, /device:TPU:1, one launch (start us, length us, event | category | flops | bytes accessed | tf_op | source)
XLA Modules:
  0.0 49.0 jit_solution(10085510708245331611)
XLA Ops:
  0.6 44.8 %shard_map.75 = (f32[128,128]{1,0:T(8,128)S(1)}, f32[128,128]{1,0:T(8,128)S(1)}, f32[16,128]{1,0:T(8,128)S(1)}, f32[1,1]{1,0:T(1,128)}) custom-call(bf16[16,128,2048]{2,1,0:T(8,128)(2,1)} %field.1, bf16[128,128]{1,0:T(8,128)(2,1)} %s_hbm.1, bf16[128,128]{1,0:T(8,128)(2,1)} %l_hbm.1, bf16[16,128]{1,0:T(8,128)(2,1)} %t_hbm.1), custom_call_target="tpu_custom_call" | custom-call | tf_op jit(solution)/shard_map/pallas_call | solution.py:420
  45.4 0.6 %copy.12 = f32[128,128]{1,0:T(8,128)} copy(f32[128,128]{1,0:T(8,128)S(1)} %get-tuple-element.16) | data formatting | bytes 131072
  46.1 0.6 %copy.13 = f32[128,128]{1,0:T(8,128)} copy(f32[128,128]{1,0:T(8,128)S(1)} %get-tuple-element.17) | data formatting | bytes 131072
  46.7 0.6 %copy.14 = f32[16,128]{1,0:T(8,128)} copy(f32[16,128]{1,0:T(8,128)S(1)} %get-tuple-element.18) | data formatting | bytes 16384

commit v6 on v5

--- a/solution.py
+++ b/solution.py
@@ -272,9 +272,6 @@
     for s in (2, 3):
         zs[s] = part[0, s] + xbuf[s]
         short(s).start()
-    rs_x1.wait_recv()
-    zs[1] = part[0, 1] + xbuf[1]
-    far().start()
 
     for k in range(1, NT):
         a1_in(k).wait_recv()
@@ -292,6 +289,9 @@
     for k in range(1, NS):
         a2(k).start()
     r2[sp] = m2[...]
+    rs_x1.wait_recv()
+    zs[1] = part[0, 1] + xbuf[1]
+    far().start()
 
     for k in range(1, NA):
         b1_in(k).wait_recv()

time: 49.1 us -> 49.2 us (level)
  the two profiles are of different devices: /device:TPU:1 before, /device:TPU:8 now
where the time goes in v6:
time: 49.2 us; the launch traced here: 49.1 us
  Pallas kernels  44.9 us (91%)
  between operations  2.33 us (5%)
  local copies, waits for them, and re-layouts  1.86 us (4%)
    pallas_call x1, Pallas kernels, on_device(): pl.pallas_call(functools.partial(kernel, scales), out_shape=(jax.ShapeDty...  44.9 us
    unnamed x3, local copies, waits for them, and re-layouts  1.86 us

profile of v6, /device:TPU:8, one launch (start us, length us, event | category | flops | bytes accessed | tf_op | source)
XLA Modules:
  0.0 49.1 jit_solution(12675557021378320541)
XLA Ops:
  0.6 44.9 %shard_map.75 = (f32[128,128]{1,0:T(8,128)S(1)}, f32[128,128]{1,0:T(8,128)S(1)}, f32[16,128]{1,0:T(8,128)S(1)}, f32[1,1]{1,0:T(1,128)}) custom-call(bf16[16,128,2048]{2,1,0:T(8,128)(2,1)} %field.1, bf16[128,128]{1,0:T(8,128)(2,1)} %s_hbm.1, bf16[128,128]{1,0:T(8,128)(2,1)} %l_hbm.1, bf16[16,128]{1,0:T(8,128)(2,1)} %t_hbm.1), custom_call_target="tpu_custom_call" | custom-call | tf_op jit(solution)/shard_map/pallas_call | solution.py:420
  45.6 0.6 %copy.12 = f32[128,128]{1,0:T(8,128)} copy(f32[128,128]{1,0:T(8,128)S(1)} %get-tuple-element.16) | data formatting | bytes 131072
  46.2 0.6 %copy.13 = f32[128,128]{1,0:T(8,128)} copy(f32[128,128]{1,0:T(8,128)S(1)} %get-tuple-element.17) | data formatting | bytes 131072
  46.8 0.6 %copy.14 = f32[16,128]{1,0:T(8,128)} copy(f32[16,128]{1,0:T(8,128)S(1)} %get-tuple-element.18) | data formatting | bytes 16384
